TPU v7x, 32 devices: a whole 2x2x4 slice. The times are simulated.
32 devices in a mesh: gx: 8 (over y, x, core), gy: 4 (over z).
Axes of the slice: x: 2, y: 2, z: 4, core: 2. Of those that a mesh axis runs over, the one named last changes fastest.
Arguments:
- u_vel: bfloat16 [128, 256, 1024], P(None, 'gx', 'gy'), may hold values from -6 to 6
- v_vel: bfloat16 [128, 256, 1024], P(None, 'gx', 'gy'), may hold values from -6 to 6
- inv_dx: float32 [256, 1024], P('gx', 'gy'), may hold values from 0.5 to 2
- inv_dy: float32 [256, 1024], P('gx', 'gy'), may hold values from 0.5 to 2
Outputs:
- recon_vorticity: bfloat16 [128, 256, 1024], P(None, 'gx', 'gy')
- recon_divergence: bfloat16 [128, 256, 1024], P(None, 'gx', 'gy')
All inputs are finite; a program needn't handle non-finite values.
Results may differ from a plain program's by a relative error of at most 0.0045.
Values may be sent and summed in bfloat16 or wider, within the bound.
A program may use at most 64 MiB of HBM per device.

v0:
```python
import jax
import jax.numpy as jnp
from jax import lax
from jax.sharding import PartitionSpec as P

ITERS = 8


def swapped(block, axis, stride):
    count = lax.axis_size(axis)
    route = []
    for low in range(count):
        high = low | 1 << stride
        if high != low and high < count:
            route += [(low, high), (high, low)]
    return lax.ppermute(block, axis, route)


def with_halo(cells, sides, width):
    for axis, dim in sides:
        count = lax.axis_size(axis)
        ends = count - 1
        head = lax.slice_in_dim(cells, 0, width, axis=dim)
        tail = lax.slice_in_dim(cells, cells.shape[dim] - width, cells.shape[dim], axis=dim)
        cells = jnp.concatenate(
            [
                lax.ppermute(tail, axis, [(i, (i + 1) % count) for i in range(ends)]),
                cells,
                lax.ppermute(head, axis, [((i + 1) % count, i) for i in range(ends)]),
            ],
            axis=dim,
        )
    return cells


def along_first(padded):
    return (
        padded[..., 0:-4, 2:-2]
        - 8.0 * padded[..., 1:-3, 2:-2]
        + 8.0 * padded[..., 3:-1, 2:-2]
        - padded[..., 4:, 2:-2]
    ) / 12.0


def along_second(padded):
    return (
        padded[..., 2:-2, 0:-4]
        - 8.0 * padded[..., 2:-2, 1:-3]
        + 8.0 * padded[..., 2:-2, 3:-1]
        - padded[..., 2:-2, 4:]
    ) / 12.0


def spectral_filter(gram_sum):
    order = gram_sum.shape[0]
    identity = jnp.eye(order, dtype=jnp.float32)
    shift = jnp.trace(gram_sum) / order
    scale = jnp.sqrt(jnp.sum(gram_sum * gram_sum))
    signum = (gram_sum - shift * identity) / scale
    for sweep in range(ITERS):
        square = jnp.dot(signum, signum, precision=lax.Precision.HIGHEST)
        cube = jnp.dot(signum, square, precision=lax.Precision.HIGHEST)
        signum = 1.5 * signum - 0.5 * cube
    return ((identity + signum) * 0.5).astype(jnp.bfloat16)


def reduce_gram(partial_gram):
    running = partial_gram
    for bit_index in range(lax.axis_size("gx").bit_length() - 1):
        running = running + swapped(running, "gx", bit_index)
    for bit_index in range(lax.axis_size("gy").bit_length() - 1):
        running = running + swapped(running, "gy", bit_index)
    return running


def per_device(u_vel, v_vel, inv_dx, inv_dy):
    snaps, tile_x, tile_y = u_vel.shape
    velocity = jnp.stack([u_vel, v_vel])
    padded = with_halo(velocity, (("gx", 2), ("gy", 3)), 2)
    pad_u = padded[0].astype(jnp.float32)
    pad_v = padded[1].astype(jnp.float32)
    vorticity = (inv_dx * along_first(pad_v) - inv_dy * along_second(pad_u)).astype(jnp.bfloat16)
    divergence = (inv_dx * along_first(pad_u) + inv_dy * along_second(pad_v)).astype(jnp.bfloat16)
    cells = tile_x * tile_y
    flat_vort = vorticity.reshape(snaps, cells)
    flat_div = divergence.reshape(snaps, cells)
    snapshots = jnp.concatenate([flat_vort, flat_div], 0)
    partial_gram = jnp.dot(snapshots, snapshots.T, preferred_element_type=jnp.float32)
    gram_sum = reduce_gram(partial_gram)
    filter_bf = spectral_filter(gram_sum)
    rebuilt = jnp.dot(filter_bf.T, snapshots, preferred_element_type=jnp.float32).astype(
        jnp.bfloat16
    )
    recon_vorticity = rebuilt[:snaps].reshape(snaps, tile_x, tile_y)
    recon_divergence = rebuilt[snaps:].reshape(snaps, tile_x, tile_y)
    return (recon_vorticity, recon_divergence)


def solution(mesh):
    in_specs = (P(None, "gx", "gy"), P(None, "gx", "gy"), P("gx", "gy"), P("gx", "gy"))
    out_specs = (P(None, "gx", "gy"), P(None, "gx", "gy"))
    return jax.shard_map(
        per_device, mesh=mesh, in_specs=in_specs, out_specs=out_specs, check_vma=False
    )
```

profile of v0, /device:TPU:0, one launch (start us, length us, event | category | flops | bytes accessed | tf_op | source)
XLA Modules:
  0.0 97.8 jit_solution(5534974748918065637)
XLA Ops:
  0.6 3.5 %copy.6 = bf16[128,32,256]{0,2,1:T(8,128)(2,1)S(1)} copy(bf16[128,32,256]{2,1,0:T(8,128)(2,1)} %param.4) | data formatting | bytes 4194304 | tf_op args[0]
  4.1 4.5 %copy.7 = bf16[128,32,256]{0,2,1:T(8,128)(2,1)} copy(bf16[128,32,256]{2,1,0:T(8,128)(2,1)} %param.5) | data formatting | bytes 4194304 | tf_op args[1]
  8.6 0.0 copy-start
  8.6 0.0 copy-start.3
  8.6 0.0 copy-start.4
  8.6 1.2 %pad_maximum_fusion.5 = (bf16[2,128,2,256]{1,3,2,0:T(8,128)(2,1)S(1)}, bf16[2,128,2,256]{1,3,2,0:T(8,128)(2,1)S(1)}) fusion(bf16[1,128,32,256]{1,3,2,0:T(8,128)(2,1)} %bitcast.51, bf16[1,128,32,256]{1,3,2,0:T(8,128)(2,1)S(1)} %bitcast.48), kind=kLoop, calls=%fused_computation.55 | loop fusion | flops 262144 | bytes 4718592 | tf_op jit(solution)/shard_map/slice | solution.py:24
  9.8 2.4 %collective-permute-start = (bf16[2,128,2,256]{1,3,2,0:T(8,128)(2,1)S(1)}, bf16[2,128,2,256]{1,3,2,0:T(8,128)(2,1)S(1)}, u32[]{:S(2)}, u32[]{:S(2)}) collective-permute-start(bf16[2,128,2,256]{1,3,2,0:T(8,128)(2,1)S(1)} %get-tuple-element.13), channel_id=1, source_target_pairs={{0,4},{4,8},{8,12},{12,16},{16,20},{20,24},{24,28},{1,5},{5,9},{9,... | collective-permute-start | bytes 786440 | tf_op jit(solution)/shard_map/ppermute | solution.py:27
  12.2 1.3 %collective-permute-start.1 = (bf16[2,128,2,256]{1,3,2,0:T(8,128)(2,1)S(1)}, bf16[2,128,2,256]{1,3,2,0:T(8,128)(2,1)S(1)}, u32[]{:S(2)}, u32[]{:S(2)}) collective-permute-start(bf16[2,128,2,256]{1,3,2,0:T(8,128)(2,1)S(1)} %get-tuple-element.14), channel_id=1, source_target_pairs={{4,0},{8,4},{12,8},{16,12},{20,16},{24,20},{28,24},{5,1},{9,5},{13... | collective-permute-start | bytes 786440 | tf_op jit(solution)/shard_map/ppermute | solution.py:29
  13.5 0.0 collective-permute-done
  13.5 4.2 %collective-permute-done.1 = bf16[2,128,2,256]{1,3,2,0:T(8,128)(2,1)S(1)} collective-permute-done((bf16[2,128,2,256]{1,3,2,0:T(8,128)(2,1)S(1)}, bf16[2,128,2,256]{1,3,2,0:T(8,128)(2,1)S(1)}, u32[]{:S(2)}, u32[]{:S(2)}) %collective-permute-start.1) | collective-permute-done | bytes 262176 | tf_op jit(solution)/shard_map/ppermute | solution.py:29
  17.7 0.0 copy-done
  17.7 0.1 pad_maximum_fusion.9
  17.8 3.5 %collective-permute-start.2 = (bf16[2,128,36,2]{1,3,2,0:T(2,128)(2,1)S(1)}, bf16[2,128,36,2]{1,3,2,0:T(2,128)(2,1)S(1)}, u32[]{:S(2)}, u32[]{:S(2)}) collective-permute-start(bf16[2,128,36,2]{1,3,2,0:T(2,128)(2,1)S(1)} %get-tuple-element.9), channel_id=1, source_target_pairs={{0,1},{1,2},{2,3},{4,5},{5,6},{6,7},{8,9},{9,10},{10,11},{12,13},{... | collective-permute-start | bytes 110600 | tf_op jit(solution)/shard_map/ppermute | solution.py:27
  21.2 1.3 %collective-permute-start.3 = (bf16[2,128,36,2]{1,3,2,0:T(2,128)(2,1)S(1)}, bf16[2,128,36,2]{1,3,2,0:T(2,128)(2,1)S(1)}, u32[]{:S(2)}, u32[]{:S(2)}) collective-permute-start(bf16[2,128,36,2]{1,3,2,0:T(2,128)(2,1)S(1)} %get-tuple-element.10), channel_id=1, source_target_pairs={{1,0},{2,1},{3,2},{5,4},{6,5},{7,6},{9,8},{10,9},{11,10},{13,12},{... | collective-permute-start | bytes 110600 | tf_op jit(solution)/shard_map/ppermute | solution.py:29
  22.5 0.0 copy-done.3
  22.6 0.0 copy-done.4
  22.6 0.3 collective-permute-done.2
  22.9 4.2 %collective-permute-done.3 = bf16[2,128,36,2]{1,3,2,0:T(2,128)(2,1)S(1)} collective-permute-done((bf16[2,128,36,2]{1,3,2,0:T(2,128)(2,1)S(1)}, bf16[2,128,36,2]{1,3,2,0:T(2,128)(2,1)S(1)}, u32[]{:S(2)}, u32[]{:S(2)}) %collective-permute-start.3) | collective-permute-done | bytes 36896 | tf_op jit(solution)/shard_map/ppermute | solution.py:29
  27.1 4.3 %pad_maximum_fusion = bf16[2,128,36,260]{1,3,2,0:T(8,128)(2,1)S(1)} fusion(bf16[2,128,36,2]{1,3,2,0:T(2,128)(2,1)S(1)} %collective-permute-done.3, bf16[2,128,2,256]{1,3,2,0:T(8,128)(2,1)S(1)} %collective-permute-done.1, bf16[1,128,32,256]{1,3,2,0:T(8,128)(2,1)S(1)} %bitcast.53, bf16[1,128,32,256]{1,3,2,0:T(8,128)(2,1)S(1)} %bitcast.50, ...), kind=kLoop, calls=%fused_computation.1 | loop fusion | flops 28753920 | bytes 9584640 | tf_op jit(solution)/shard_map/concatenate | solution.py:25
  31.4 0.7 fusion.17
  32.1 8.4 %fusion.10 = (bf16[128,32,256]{0,2,1:T(8,128)(2,1)S(1)}, bf16[128,32,256]{0,2,1:T(8,128)(2,1)S(1)}) fusion(f32[128,36,260]{0,2,1:T(8,128)S(1)} %get-tuple-element.7, f32[128,36,260]{0,2,1:T(8,128)S(1)} %get-tuple-element.8, f32[32,256]{1,0:T(8,128)S(1)} %get-tuple-element.15, f32[32,256]{1,0:T(8,128)S(1)} %get-tuple-element.16), kind=kLoop, calls=%fused_computation.19 | loop fusion | flops 29360128 | bytes 71368704 | tf_op jit(solution)/shard_map/convert_element_type | solution.py:82
  40.5 0.0 copy-start.1
  40.5 1.3 %fusion.16 = f32[256,256]{1,0:T(8,128)S(1)} fusion(bf16[128,8192]{0,1:T(8,128)(2,1)S(1)} %bitcast.58, bf16[128,8192]{0,1:T(8,128)(2,1)S(1)} %bitcast.56), kind=kOutput, calls=%fused_computation.31 | convolution fusion | flops 1082130432 | bytes 4456448 | tf_op jit(solution)/shard_map/dot_general | solution.py:88
  41.8 0.0 copy-done.1
  41.9 3.5 %collective-permute-start.4 = (f32[256,256]{1,0:T(8,128)S(1)}, f32[256,256]{1,0:T(8,128)S(1)}, u32[]{:S(2)}, u32[]{:S(2)}) collective-permute-start(f32[256,256]{1,0:T(8,128)S(1)} %fusion.16), channel_id=1, source_target_pairs={{0,4},{4,0},{8,12},{12,8},{16,20},{20,16},{24,28},{28,24},{1,5},{5... | collective-permute-start | bytes 786440 | tf_op jit(solution)/shard_map/ppermute | solution.py:16
  45.3 1.2 %collective-permute-done.4 = f32[256,256]{1,0:T(8,128)S(1)} collective-permute-done((f32[256,256]{1,0:T(8,128)S(1)}, f32[256,256]{1,0:T(8,128)S(1)}, u32[]{:S(2)}, u32[]{:S(2)}) %collective-permute-start.4) | collective-permute-done | bytes 262176 | tf_op jit(solution)/shard_map/ppermute | solution.py:16
  46.5 2.4 %collective-permute-start.5 = (f32[256,256]{1,0:T(8,128)S(1)}, f32[256,256]{1,0:T(8,128)S(1)}, u32[]{:S(2)}, u32[]{:S(2)}) collective-permute-start(f32[256,256]{1,0:T(8,128)S(1)} %add.38), channel_id=1, source_target_pairs={{0,8},{8,0},{4,12},{12,4},{16,24},{24,16},{20,28},{28,20},{1,9},{9... | collective-permute-start | bytes 786440 | tf_op jit(solution)/shard_map/ppermute | solution.py:16
  48.9 6.8 %collective-permute-done.5 = f32[256,256]{1,0:T(8,128)S(1)} collective-permute-done((f32[256,256]{1,0:T(8,128)S(1)}, f32[256,256]{1,0:T(8,128)S(1)}, u32[]{:S(2)}, u32[]{:S(2)}) %collective-permute-start.5) | collective-permute-done | bytes 262176 | tf_op jit(solution)/shard_map/ppermute | solution.py:16
  55.8 1.6 %collective-permute-start.6 = (f32[256,256]{1,0:T(8,128)S(1)}, f32[256,256]{1,0:T(8,128)S(1)}, u32[]{:S(2)}, u32[]{:S(2)}) collective-permute-start(f32[256,256]{1,0:T(8,128)S(1)} %add.39), channel_id=1, source_target_pairs={{0,16},{16,0},{4,20},{20,4},{8,24},{24,8},{12,28},{28,12},{1,17},{... | collective-permute-start | bytes 786440 | tf_op jit(solution)/shard_map/ppermute | solution.py:16
  57.4 6.4 %collective-permute-done.6 = f32[256,256]{1,0:T(8,128)S(1)} collective-permute-done((f32[256,256]{1,0:T(8,128)S(1)}, f32[256,256]{1,0:T(8,128)S(1)}, u32[]{:S(2)}, u32[]{:S(2)}) %collective-permute-start.6) | collective-permute-done | bytes 262176 | tf_op jit(solution)/shard_map/ppermute | solution.py:16
  63.9 1.6 %collective-permute-start.7 = (f32[256,256]{1,0:T(8,128)S(1)}, f32[256,256]{1,0:T(8,128)S(1)}, u32[]{:S(2)}, u32[]{:S(2)}) collective-permute-start(f32[256,256]{1,0:T(8,128)S(1)} %add.40), channel_id=1, source_target_pairs={{0,1},{1,0},{2,3},{3,2},{4,5},{5,4},{6,7},{7,6},{8,9},{9,8},{10,11... | collective-permute-start | bytes 786440 | tf_op jit(solution)/shard_map/ppermute | solution.py:16
  65.5 5.6 %collective-permute-done.7 = f32[256,256]{1,0:T(8,128)S(1)} collective-permute-done((f32[256,256]{1,0:T(8,128)S(1)}, f32[256,256]{1,0:T(8,128)S(1)}, u32[]{:S(2)}, u32[]{:S(2)}) %collective-permute-start.7) | collective-permute-done | bytes 262176 | tf_op jit(solution)/shard_map/ppermute | solution.py:16
  71.1 2.7 %collective-permute-start.8 = (f32[256,256]{1,0:T(8,128)S(1)}, f32[256,256]{1,0:T(8,128)S(1)}, u32[]{:S(2)}, u32[]{:S(2)}) collective-permute-start(f32[256,256]{1,0:T(8,128)S(1)} %add.41), channel_id=1, source_target_pairs={{0,2},{2,0},{1,3},{3,1},{4,6},{6,4},{5,7},{7,5},{8,10},{10,8},{9,1... | collective-permute-start | bytes 786440 | tf_op jit(solution)/shard_map/ppermute | solution.py:16
  73.8 10.1 %collective-permute-done.8 = f32[256,256]{1,0:T(8,128)S(1)} collective-permute-done((f32[256,256]{1,0:T(8,128)S(1)}, f32[256,256]{1,0:T(8,128)S(1)}, u32[]{:S(2)}, u32[]{:S(2)}) %collective-permute-start.8) | collective-permute-done | bytes 262176 | tf_op jit(solution)/shard_map/ppermute | solution.py:16
  83.9 0.7 select_reduce_fusion
  86.0 0.4 fusion.29
  86.4 0.4 multiply_subtract_fusion
  86.8 0.4 fusion.35
  87.2 0.4 fusion.25
  87.6 0.4 fusion.36
  88.0 0.0 copy-start.2
  88.0 0.4 fusion.24
  88.4 0.4 fusion.37
  88.8 0.4 fusion.23
  89.1 0.4 fusion.38
  89.5 0.4 fusion.22
  89.9 0.4 fusion.39
  90.3 0.4 fusion.21
  90.7 0.4 fusion.40
  91.1 0.4 fusion.20
  91.5 0.4 fusion.41
  91.9 0.4 fusion.28
  92.3 0.0 copy-done.2
  92.3 1.3 %convolution_convert_fusion = bf16[256,8192]{1,0:T(8,128)(2,1)S(1)} fusion(bf16[256,256]{1,0:T(8,128)(2,1)S(1)} %fusion.28, bf16[128,8192]{0,1:T(8,128)(2,1)S(1)} %bitcast.59, bf16[128,8192]{0,1:T(8,128)(2,1)S(1)} %bitcast.57), kind=kOutput, calls=%fused_computation | convolution fusion | flops 1084227584 | bytes 8519680 | tf_op jit(solution)/shard_map/dot_general | solution.py:91
  93.6 0.3 fusion.34
  94.0 1.9 %copy.9 = bf16[16,8,32,256]{3,2,1,0:T(8,128)(2,1)} copy(bf16[16,8,32,256]{3,1,2,0:T(8,128)(2,1)S(1)} %bitcast.55) | data formatting | bytes 4194304
  95.9 1.9 %copy.8 = bf16[16,8,32,256]{3,2,1,0:T(8,128)(2,1)} copy(bf16[16,8,32,256]{3,1,2,0:T(8,128)(2,1)S(1)} %bitcast.54) | data formatting | bytes 4194304
  (5 shorter events, 0.1 us)
Async XLA Ops:
  8.6 9.1 %copy-start = (bf16[128,32,256]{0,2,1:T(8,128)(2,1)S(1)}, bf16[128,32,256]{0,2,1:T(8,128)(2,1)}, u32[]{:S(2)}) copy-start(bf16[128,32,256]{0,2,1:T(8,128)(2,1)} %copy.7) | copy-start | bytes 6291460
  8.6 13.9 %copy-start.3 = (f32[32,256]{1,0:T(8,128)S(1)}, f32[32,256]{1,0:T(8,128)}, u32[]{:S(2)}) copy-start(f32[32,256]{1,0:T(8,128)} %param.7) | copy-start | bytes 98308
  8.6 13.9 %copy-start.4 = (f32[32,256]{1,0:T(8,128)S(1)}, f32[32,256]{1,0:T(8,128)}, u32[]{:S(2)}) copy-start(f32[32,256]{1,0:T(8,128)} %param.6) | copy-start | bytes 98308
  9.8 3.7 %collective-permute-start = (bf16[2,128,2,256]{1,3,2,0:T(8,128)(2,1)S(1)}, bf16[2,128,2,256]{1,3,2,0:T(8,128)(2,1)S(1)}, u32[]{:S(2)}, u32[]{:S(2)}) collective-permute-start(bf16[2,128,2,256]{1,3,2,0:T(8,128)(2,1)S(1)} %get-tuple-element.13), channel_id=1, source_target_pairs={{0,4},{4,8},{8,12},{12,16},{16,20},{20,24},{24,28},{1,5},{5,9},{9,... | collective-permute-start | bytes 786440 | tf_op jit(solution)/shard_map/ppermute | solution.py:27
  12.2 5.5 %collective-permute-start.1 = (bf16[2,128,2,256]{1,3,2,0:T(8,128)(2,1)S(1)}, bf16[2,128,2,256]{1,3,2,0:T(8,128)(2,1)S(1)}, u32[]{:S(2)}, u32[]{:S(2)}) collective-permute-start(bf16[2,128,2,256]{1,3,2,0:T(8,128)(2,1)S(1)} %get-tuple-element.14), channel_id=1, source_target_pairs={{4,0},{8,4},{12,8},{16,12},{20,16},{24,20},{28,24},{5,1},{9,5},{13... | collective-permute-start | bytes 786440 | tf_op jit(solution)/shard_map/ppermute | solution.py:29
  17.8 5.1 %collective-permute-start.2 = (bf16[2,128,36,2]{1,3,2,0:T(2,128)(2,1)S(1)}, bf16[2,128,36,2]{1,3,2,0:T(2,128)(2,1)S(1)}, u32[]{:S(2)}, u32[]{:S(2)}) collective-permute-start(bf16[2,128,36,2]{1,3,2,0:T(2,128)(2,1)S(1)} %get-tuple-element.9), channel_id=1, source_target_pairs={{0,1},{1,2},{2,3},{4,5},{5,6},{6,7},{8,9},{9,10},{10,11},{12,13},{... | collective-permute-start | bytes 110600 | tf_op jit(solution)/shard_map/ppermute | solution.py:27
  21.2 5.9 %collective-permute-start.3 = (bf16[2,128,36,2]{1,3,2,0:T(2,128)(2,1)S(1)}, bf16[2,128,36,2]{1,3,2,0:T(2,128)(2,1)S(1)}, u32[]{:S(2)}, u32[]{:S(2)}) collective-permute-start(bf16[2,128,36,2]{1,3,2,0:T(2,128)(2,1)S(1)} %get-tuple-element.10), channel_id=1, source_target_pairs={{1,0},{2,1},{3,2},{5,4},{6,5},{7,6},{9,8},{10,9},{11,10},{13,12},{... | collective-permute-start | bytes 110600 | tf_op jit(solution)/shard_map/ppermute | solution.py:29
  40.5 1.3 %copy-start.1 = (bf16[128,32,256]{0,2,1:T(8,128)(2,1)}, bf16[128,32,256]{0,2,1:T(8,128)(2,1)S(1)}, u32[]{:S(2)}) copy-start(bf16[128,32,256]{0,2,1:T(8,128)(2,1)S(1)} %get-tuple-element.6) | copy-start | bytes 6291460
  41.9 4.6 %collective-permute-start.4 = (f32[256,256]{1,0:T(8,128)S(1)}, f32[256,256]{1,0:T(8,128)S(1)}, u32[]{:S(2)}, u32[]{:S(2)}) collective-permute-start(f32[256,256]{1,0:T(8,128)S(1)} %fusion.16), channel_id=1, source_target_pairs={{0,4},{4,0},{8,12},{12,8},{16,20},{20,16},{24,28},{28,24},{1,5},{5... | collective-permute-start | bytes 786440 | tf_op jit(solution)/shard_map/ppermute | solution.py:16
  46.5 9.2 %collective-permute-start.5 = (f32[256,256]{1,0:T(8,128)S(1)}, f32[256,256]{1,0:T(8,128)S(1)}, u32[]{:S(2)}, u32[]{:S(2)}) collective-permute-start(f32[256,256]{1,0:T(8,128)S(1)} %add.38), channel_id=1, source_target_pairs={{0,8},{8,0},{4,12},{12,4},{16,24},{24,16},{20,28},{28,20},{1,9},{9... | collective-permute-start | bytes 786440 | tf_op jit(solution)/shard_map/ppermute | solution.py:16
  55.8 8.1 %collective-permute-start.6 = (f32[256,256]{1,0:T(8,128)S(1)}, f32[256,256]{1,0:T(8,128)S(1)}, u32[]{:S(2)}, u32[]{:S(2)}) collective-permute-start(f32[256,256]{1,0:T(8,128)S(1)} %add.39), channel_id=1, source_target_pairs={{0,16},{16,0},{4,20},{20,4},{8,24},{24,8},{12,28},{28,12},{1,17},{... | collective-permute-start | bytes 786440 | tf_op jit(solution)/shard_map/ppermute | solution.py:16
  63.9 7.2 %collective-permute-start.7 = (f32[256,256]{1,0:T(8,128)S(1)}, f32[256,256]{1,0:T(8,128)S(1)}, u32[]{:S(2)}, u32[]{:S(2)}) collective-permute-start(f32[256,256]{1,0:T(8,128)S(1)} %add.40), channel_id=1, source_target_pairs={{0,1},{1,0},{2,3},{3,2},{4,5},{5,4},{6,7},{7,6},{8,9},{9,8},{10,11... | collective-permute-start | bytes 786440 | tf_op jit(solution)/shard_map/ppermute | solution.py:16
  71.1 12.8 %collective-permute-start.8 = (f32[256,256]{1,0:T(8,128)S(1)}, f32[256,256]{1,0:T(8,128)S(1)}, u32[]{:S(2)}, u32[]{:S(2)}) collective-permute-start(f32[256,256]{1,0:T(8,128)S(1)} %add.41), channel_id=1, source_target_pairs={{0,2},{2,0},{1,3},{3,1},{4,6},{6,4},{5,7},{7,5},{8,10},{10,8},{9,1... | collective-permute-start | bytes 786440 | tf_op jit(solution)/shard_map/ppermute | solution.py:16
  88.0 4.3 %copy-start.2 = (bf16[128,32,256]{0,2,1:T(8,128)(2,1)S(1)}, bf16[128,32,256]{0,2,1:T(8,128)(2,1)}, u32[]{:S(2)}) copy-start(bf16[128,32,256]{0,2,1:T(8,128)(2,1)} %copy-done.1) | copy-start | bytes 6291460
where the time goes:
time: 98.2 us; the launch traced here: 97.8 us
  waiting for transfers between devices  38.8 us (40%)
  starting transfers between devices  20.3 us (21%)
  other arithmetic  15.5 us (16%)
  local copies, waits for them, and re-layouts  12.2 us (12%)
  matrix products  8.8 us (9%)
  between operations  2.25 us (2%)
    ppermute x5, waiting for transfers between devices, swapped(): return lax.ppermute(block, axis, route)  30.1 us
    unnamed x14, local copies, waits for them, and re-layouts  11.9 us
    ppermute x5, starting transfers between devices, swapped(): return lax.ppermute(block, axis, route)  11.8 us
    ppermute x2, waiting for transfers between devices, with_halo(): lax.ppermute(head, axis, [((i + 1) % count, i) for i in range(ends)])  8.45 us
    convert_element_type x1, other arithmetic, per_device(): (inv_dx * along_first(pad_v) - inv_dy * along_second(pad_u)).astype(jnp.b...  8.39 us
    ppermute x2, starting transfers between devices, with_halo(): lax.ppermute(tail, axis, [(i, (i + 1) % count) for i in range(ends)])  5.86 us
    concatenate x1, other arithmetic, with_halo(): jnp.concatenate([lax.ppermute(tail, axis, [(i, (i + 1) % count) for i in...  4.31 us
    dot_general x8, matrix products, spectral_filter(): cube = jnp.dot(signum, square, precision=lax.Precision.HIGHEST)  3.09 us
  transfers between devices with their start and end apart: 9, of which 8 were waited for; matrix products, arithmetic and copies ran while one was open for 0% of the time, Pallas kernels for 0%

commit v1 on v0

v1 whole, which is shorter than its diff:
```python
import functools

import jax
import jax.numpy as jnp
from jax import lax
from jax.experimental import pallas as pl
from jax.experimental.pallas import tpu as pltpu
from jax.sharding import PartitionSpec as P

ITERS = 8
EDGE = 2
SUB = 16
BATCH = 4
F32 = jnp.float32
BF16 = jnp.bfloat16
MESH = pl.DeviceIdType.MESH


def iota(shape, dim):
    return lax.broadcasted_iota(jnp.int32, shape, dim)


def swap_matrix():
    size = SUB * SUB
    row, col = iota((size, size), 0), iota((size, size), 1)
    hit = (row // SUB == col % SUB) & (row % SUB == col // SUB)
    return hit.astype(F32).astype(BF16)


def stencil_weight(gap):
    return jnp.where(
        gap == -2,
        1.0,
        jnp.where(gap == -1, -8.0, jnp.where(gap == 1, 8.0, jnp.where(gap == 2, -1.0, 0.0))),
    ).astype(BF16)


def dot(a, b):
    return jnp.dot(a, b, preferred_element_type=F32)


def dot_nt(a, b):
    return lax.dot_general(a, b, (((1,), (1,)), ((), ())), preferred_element_type=F32)


def split(x):
    high = x.astype(BF16)
    return high, (x - high.astype(F32)).astype(BF16)


def product(a, b):
    (ah, al), (bh, bl) = a, b
    return dot(
        jnp.concatenate([ah, al, ah], axis=1), jnp.concatenate([bh, bh, bl], axis=0)
    )


def spectral_filter(gram):
    order = gram.shape[0]
    eye = iota((order, order), 0) == iota((order, order), 1)

    def total(x):
        return jnp.sum(jnp.sum(x, axis=0, keepdims=True), axis=1, keepdims=True)

    shift = total(jnp.where(eye, gram, 0.0)) / order
    scale = jnp.sqrt(total(gram * gram))
    signum = (gram - jnp.where(eye, shift, 0.0)) / scale
    for sweep in range(ITERS):
        parts = split(signum)
        square = product(parts, parts)
        cube = product(parts, split(square))
        signum = 1.5 * signum - 0.5 * cube
    return ((jnp.where(eye, 1.0, 0.0) + signum) * 0.5).astype(BF16)


def pack_gram(gram, rows, count):
    half = gram.shape[0] // 2
    first, cross, second = gram[:half, :half], gram[:half, half:], gram[half:, half:]
    row, col = iota((half, half), 0), iota((half, half), 1)
    mix = jnp.where(row <= col, first, second)
    diag = jnp.sum(jnp.where(row == col, second, 0.0), axis=0, keepdims=True)
    diag = jnp.where(iota((8, half), 0) == 0, diag, 0.0)
    pad = rows * count - 2 * half - 8
    pieces = [cross, mix, diag]
    if pad:
        pieces.append(jnp.zeros((pad, half), F32))
    return jnp.concatenate(pieces, axis=0).reshape(count, rows, half)


def unpack_gram(packed):
    half = packed.shape[-1]
    flat = packed.reshape(-1, half)
    cross, mix = flat[:half], flat[half : 2 * half]
    diag = flat[2 * half : 2 * half + 1]
    row, col = iota((half, half), 0), iota((half, half), 1)
    flipped = mix.T
    first = jnp.where(row <= col, mix, flipped)
    second = jnp.where(row == col, diag, jnp.where(row > col, mix, flipped))
    top = jnp.concatenate([first, cross], axis=1)
    bottom = jnp.concatenate([cross.T, second], axis=1)
    return jnp.concatenate([top, bottom], axis=0)


def filter_kernel(
    n_gx, n_gy, snaps, tile_x, tile_y, rows,
    u_hbm, v_hbm, idx_hbm, idy_hbm,
    s_hbm, filter_ref,
    uv, inv, field, snap, strip, strip_low, strip_high, gram,
    packed, reduce_buf, z_buf, full,
    load_sem, store_sem, x_send, x_recv, y_send, y_recv,
    rs_send, rs_recv, z_send, z_recv, ag_send, ag_recv,
):
    gx, gy = lax.axis_index("gx"), lax.axis_index("gy")
    lanes = strip.shape[1]

    loads = [
        pltpu.make_async_copy(source, target, load_sem.at[i])
        for i, (source, target) in enumerate(
            [(u_hbm, uv.at[0]), (v_hbm, uv.at[1]), (idx_hbm, inv.at[0]), (idy_hbm, inv.at[1])]
        )
    ]
    for load in loads:
        load.start()

    barrier = pltpu.get_barrier_semaphore()
    for k in range(1, n_gx):
        pl.semaphore_signal(
            barrier, inc=1, device_id={"gx": lax.rem(gx + k, n_gx)}, device_id_type=MESH
        )
    for k in range(1, n_gy):
        pl.semaphore_signal(
            barrier, inc=1, device_id={"gy": lax.rem(gy + k, n_gy)}, device_id_type=MESH
        )

    def x_copy(comp, up):
        span = pl.ds(comp * snaps, snaps)
        src = field.at[pl.ds(tile_x if up else EDGE, EDGE), span]
        dst = field.at[pl.ds(0 if up else tile_x + EDGE, EDGE), span]
        return pltpu.make_async_remote_copy(
            src_ref=src, dst_ref=dst,
            send_sem=x_send.at[comp, up], recv_sem=x_recv.at[comp, up],
            device_id={"gx": gx + 1 if up else gx - 1}, device_id_type=MESH,
        )

    def y_copy(comp, up):
        span = pl.ds(comp * snaps, snaps)
        dst = strip_low if up else strip_high
        return pltpu.make_async_remote_copy(
            src_ref=strip.at[span], dst_ref=dst.at[span],
            send_sem=y_send.at[comp, up], recv_sem=y_recv.at[comp, up],
            device_id={"gy": gy + 1 if up else gy - 1}, device_id_type=MESH,
        )

    def has(index, count, up):
        return index < count - 1 if up else index > 0

    swap = swap_matrix()
    lane = iota((tile_y, lanes), 1)
    column = jnp.where(lane >= lanes // 2, tile_y - EDGE, 0) + lane % EDGE
    pick = (iota((tile_y, lanes), 0) == column).astype(F32).astype(BF16)
    group = (SUB, SUB, lanes)
    lane_x = (iota(group, 2) % (lanes // 2)) // EDGE - iota(group, 0)

    def permute(comp, j):
        first = pl.multiple_of(j * SUB, SUB)
        there = pl.multiple_of(comp * snaps + j * SUB, SUB)
        edge = jnp.zeros((SUB, lanes), F32)
        for x0 in range(0, tile_x, SUB):
            block = uv[comp, pl.ds(first, SUB), x0 : x0 + SUB, :]
            moved = dot(swap, block.reshape(SUB * SUB, tile_y)).astype(BF16)
            field[EDGE + x0 : EDGE + x0 + SUB, pl.ds(there, SUB), :] = moved.reshape(
                SUB, SUB, tile_y
            )
            taken = dot(moved, pick).reshape(group)
            edge = edge + jnp.sum(jnp.where(lane_x == x0, taken, 0.0), axis=0)
        strip[pl.ds(there, SUB), :] = edge.astype(BF16)

    for comp in range(2):
        loads[comp].wait()

        def permute_some(step, carry, comp=comp):
            for i in range(BATCH):
                permute(comp, step * BATCH + i)
            return carry

        lax.fori_loop(0, snaps // SUB // BATCH, permute_some, 0)
        if comp == 0:
            pl.semaphore_wait(barrier, n_gx + n_gy - 2)
        for up in range(2):
            @pl.when(has(gy, n_gy, up))
            def _(comp=comp, up=up):
                y_copy(comp, up).start()

            @pl.when(has(gx, n_gx, up))
            def _(comp=comp, up=up):
                x_copy(comp, up).start()

    @pl.when(gx == 0)
    def _():
        field[0:EDGE] = jnp.zeros((EDGE, 2 * snaps, tile_y), BF16)

    @pl.when(gx == n_gx - 1)
    def _():
        field[tile_x + EDGE :] = jnp.zeros((EDGE, 2 * snaps, tile_y), BF16)

    @pl.when(gy == 0)
    def _():
        strip_low[...] = jnp.zeros((2 * snaps, lanes), BF16)

    @pl.when(gy == n_gy - 1)
    def _():
        strip_high[...] = jnp.zeros((2 * snaps, lanes), BF16)

    for load in loads[2:]:
        load.wait()
    inv[...] = inv[...] * (1.0 / 12.0)
    gram[...] = jnp.zeros_like(gram)
    within = stencil_weight(iota((tile_y, tile_y), 0) - iota((tile_y, tile_y), 1))
    spot = iota((lanes, tile_y), 0)
    outer = jnp.where(spot >= lanes // 2, -EDGE, tile_y) + spot % EDGE
    beyond = stencil_weight(outer - iota((lanes, tile_y), 1))

    def wait_arrivals(copy, index, count):
        for comp in range(2):
            for up in range(2):
                @pl.when(has(index, count, 1 - up))
                def _(comp=comp, up=up):
                    copy(comp, up).wait_recv()

    wait_arrivals(y_copy, gy, n_gy)
    wide = (2 * snaps, lanes)
    halo = jnp.where(
        iota(wide, 1) >= lanes // 2, strip_low[...].astype(F32), strip_high[...].astype(F32)
    )
    strip_low[...] = halo.astype(BF16)
    owner = (iota(wide, 1) % (lanes // 2)) // EDGE

    def fields(x0, count):
        middle = field[pl.ds(x0 + EDGE, count)].reshape(count * 2 * snaps, tile_y)
        side = strip_low[...].astype(F32)
        sides = [jnp.where(owner == x0 + i, side, 0.0).astype(BF16) for i in range(count)]
        along_y = dot(middle, within) + dot(jnp.concatenate(sides, axis=0), beyond)
        done = []
        for i in range(count):
            near = field[x0 + i + 3].astype(F32) - field[x0 + i + 1].astype(F32)
            far = field[x0 + i].astype(F32) - field[x0 + i + 4].astype(F32)
            along_x = far + 8.0 * near
            at = along_y[i * 2 * snaps : (i + 1) * 2 * snaps]
            idx, idy = inv[0, pl.ds(x0 + i, 1), :], inv[1, pl.ds(x0 + i, 1), :]
            vorticity = idx * along_x[snaps:] - idy * at[:snaps]
            divergence = idx * along_x[:snaps] + idy * at[snaps:]
            both = jnp.concatenate([vorticity, divergence], axis=0).astype(BF16)
            snap[x0 + i] = both
            done.append(both)
        flat = jnp.concatenate(done, axis=1)
        gram[...] += dot_nt(flat, flat)

    def interior(step, carry):
        fields(EDGE + step * BATCH, BATCH)
        return carry

    lax.fori_loop(0, (tile_x - 2 * EDGE) // BATCH, interior, 0)
    wait_arrivals(x_copy, gx, n_gx)
    fields(0, EDGE)
    fields(tile_x - EDGE, EDGE)

    store = pltpu.make_async_copy(snap, s_hbm, store_sem)
    store.start()

    packed[...] = pack_gram(gram[...], rows, n_gx)

    def rs_copy(k):
        peer = lax.rem(gx + k, n_gx)
        return pltpu.make_async_remote_copy(
            src_ref=packed.at[peer], dst_ref=reduce_buf.at[k],
            send_sem=rs_send.at[k], recv_sem=rs_recv.at[k],
            device_id={"gx": peer}, device_id_type=MESH,
        )

    def z_copy(k):
        return pltpu.make_async_remote_copy(
            src_ref=z_buf.at[0], dst_ref=z_buf.at[k],
            send_sem=z_send.at[k], recv_sem=z_recv.at[k],
            device_id={"gy": lax.rem(gy + k, n_gy)}, device_id_type=MESH,
        )

    def ag_copy(k, block):
        return pltpu.make_async_remote_copy(
            src_ref=full.at[block], dst_ref=full.at[block],
            send_sem=ag_send.at[k], recv_sem=ag_recv.at[k],
            device_id={"gx": lax.rem(gx + k, n_gx)}, device_id_type=MESH,
        )

    for k in range(1, n_gx):
        rs_copy(k).start()
    mine = packed[gx]
    for k in range(1, n_gx):
        rs_copy(k).wait_recv()
        mine = mine + reduce_buf[k]
    z_buf[0] = mine
    for k in range(1, n_gy):
        z_copy(k).start()
    for k in range(1, n_gy):
        z_copy(k).wait_recv()
    total = z_buf[lax.rem(gy, n_gy)]
    for z in range(1, n_gy):
        total = total + z_buf[lax.rem(gy - z + n_gy, n_gy)]
    full[gx] = total
    for k in range(1, n_gx):
        ag_copy(k, gx).start()
    for k in range(1, n_gx):
        ag_copy(k, lax.rem(gx - k + n_gx, n_gx)).wait_recv()

    filter_ref[...] = spectral_filter(unpack_gram(full[...]))

    for comp in range(2):
        for up in range(2):
            @pl.when(has(gy, n_gy, up))
            def _(comp=comp, up=up):
                y_copy(comp, up).wait_send()

            @pl.when(has(gx, n_gx, up))
            def _(comp=comp, up=up):
                x_copy(comp, up).wait_send()
    for k in range(1, n_gx):
        rs_copy(k).wait_send()
        ag_copy(k, gx).wait_send()
    for k in range(1, n_gy):
        z_copy(k).wait_send()
    store.wait()


def rebuild_kernel(s_ref, filter_ref, vort_ref, div_ref, mixed):
    count, order, tile_y = s_ref.shape
    half = order // 2
    for x in range(count):
        mixed[x] = dot(filter_ref[...], s_ref[x]).astype(BF16)
    swap = swap_matrix()
    for first in range(0, order, SUB):
        block = mixed[:, first : first + SUB, :].reshape(SUB * SUB, tile_y)
        back = dot(swap, block).astype(BF16).reshape(SUB, SUB, tile_y)
        out = vort_ref if first < half else div_ref
        start = first % half
        out[start : start + SUB] = back


def per_device(n_gx, n_gy, u_vel, v_vel, inv_dx, inv_dy):
    snaps, tile_x, tile_y = u_vel.shape
    order = 2 * snaps
    lanes = 2 * EDGE * tile_x
    rows = -(-(order + 8) // (8 * n_gx)) * 8
    any_spec = pl.BlockSpec(memory_space=pl.ANY)
    dma = pltpu.SemaphoreType.DMA
    snapshots, spectral = pl.pallas_call(
        functools.partial(filter_kernel, n_gx, n_gy, snaps, tile_x, tile_y, rows),
        out_shape=(
            jax.ShapeDtypeStruct((tile_x, order, tile_y), BF16),
            jax.ShapeDtypeStruct((order, order), BF16),
        ),
        in_specs=[any_spec] * 4,
        out_specs=(any_spec, pl.BlockSpec(memory_space=pltpu.VMEM)),
        scratch_shapes=[
            pltpu.VMEM((2, snaps, tile_x, tile_y), BF16),
            pltpu.VMEM((2, tile_x, tile_y), F32),
            pltpu.VMEM((tile_x + 2 * EDGE, order, tile_y), BF16),
            pltpu.VMEM((tile_x, order, tile_y), BF16),
            pltpu.VMEM((order, lanes), BF16),
            pltpu.VMEM((order, lanes), BF16),
            pltpu.VMEM((order, lanes), BF16),
            pltpu.VMEM((order, order), F32),
            pltpu.VMEM((n_gx, rows, snaps), F32),
            pltpu.VMEM((n_gx, rows, snaps), F32),
            pltpu.VMEM((n_gy, rows, snaps), F32),
            pltpu.VMEM((n_gx, rows, snaps), F32),
            dma((4,)),
            dma,
            dma((2, 2)),
            dma((2, 2)),
            dma((2, 2)),
            dma((2, 2)),
            dma((n_gx,)),
            dma((n_gx,)),
            dma((n_gy,)),
            dma((n_gy,)),
            dma((n_gx,)),
            dma((n_gx,)),
        ],
        compiler_params=pltpu.CompilerParams(
            collective_id=0, has_side_effects=True, vmem_limit_bytes=40 * 2**20
        ),
        name="filter",
    )(u_vel, v_vel, inv_dx, inv_dy)
    out = jax.ShapeDtypeStruct((snaps, tile_x, tile_y), BF16)
    block = pl.BlockSpec((snaps, SUB, tile_y), lambda i: (0, i, 0))
    return pl.pallas_call(
        rebuild_kernel,
        out_shape=(out, out),
        grid=(tile_x // SUB,),
        in_specs=[
            pl.BlockSpec((SUB, order, tile_y), lambda i: (i, 0, 0)),
            pl.BlockSpec((order, order), lambda i: (0, 0)),
        ],
        out_specs=(block, block),
        scratch_shapes=[pltpu.VMEM((SUB, order, tile_y), BF16)],
        compiler_params=pltpu.CompilerParams(vmem_limit_bytes=40 * 2**20),
        name="rebuild",
    )(snapshots, spectral)


def solution(mesh):
    in_specs = (P(None, "gx", "gy"), P(None, "gx", "gy"), P("gx", "gy"), P("gx", "gy"))
    out_specs = (P(None, "gx", "gy"), P(None, "gx", "gy"))
    return jax.shard_map(
        functools.partial(per_device, mesh.shape["gx"], mesh.shape["gy"]),
        mesh=mesh, in_specs=in_specs, out_specs=out_specs, check_vma=False,
    )
```

time: 98.2 us -> 44.5 us (0.45)
  Pallas kernels: 0 us -> 38.9 us
  waiting for transfers between devices: 38.8 us -> 0 us
  starting transfers between devices: 20.3 us -> 0 us
  other arithmetic: 15.5 us -> 0 us
  matrix products: 8.8 us -> 0 us
  local copies, waits for them, and re-layouts: 12.2 us -> 4.69 us
  between operations: 2.25 us -> 0.65 us
    pallas_call x0 -> x2, Pallas kernels: none -> 38.9 us  [the longest x1 34.8 us: per_device(): pl.pallas_call(functools.partial(filter_kernel, n_gx, n_gy, snaps, tile_x...]
    ppermute x9 -> x0, waiting for transfers between devices: 38.8 us -> none  [the longest x5 30.1 us: swapped(): return lax.ppermute(block, axis, route)]
    ppermute x9 -> x0, starting transfers between devices: 20.3 us -> none  [the longest x5 11.8 us: swapped(): return lax.ppermute(block, axis, route)]
    convert_element_type x2 -> x0, other arithmetic: 9.09 us -> none  [the longest x1 8.39 us: per_device(): (inv_dx * along_first(pad_v) - inv_dy * along_second(pad_u)).astype(jnp.b...]
    dot_general x18 -> x0, matrix products: 8.8 us -> none  [the longest x8 3.09 us: spectral_filter(): cube = jnp.dot(signum, square, precision=lax.Precision.HIGHEST)]
    unnamed x14 -> x8, local copies, waits for them, and re-layouts: 11.9 us -> 4.69 us
    concatenate x1 -> x0, other arithmetic: 4.31 us -> none  [with_halo(): jnp.concatenate([lax.ppermute(tail, axis, [(i, (i + 1) % count) for i in...]
    slice x2 -> x0, other arithmetic: 1.22 us -> none  [with_halo(): lax.slice_in_dim(cells, cells.shape[dim] - width, cells.shape[dim], axis=...]
  transfers between devices with their start and end apart: 9 -> 0, of which waited for: 8 -> 0; matrix products, arithmetic and copies ran while one was open for 0% -> 0% of each run, Pallas kernels for 0% -> 0%
where the time goes in v1:
time: 44.5 us; the launch traced here: 44.2 us
  Pallas kernels  38.9 us (87%)
  local copies, waits for them, and re-layouts  4.69 us (11%)
  between operations  0.65 us (1%)
    pallas_call x1, Pallas kernels, per_device(): pl.pallas_call(functools.partial(filter_kernel, n_gx, n_gy, snaps, tile_x...  34.8 us
    unnamed x8, local copies, waits for them, and re-layouts  4.69 us
    pallas_call x1, Pallas kernels, per_device(): pl.pallas_call(rebuild_kernel, out_shape=(out, out), grid=(tile_x // SUB,...  4.07 us

profile of v1, /device:TPU:0, one launch (start us, length us, event | category | flops | bytes accessed | tf_op | source)
XLA Modules:
  0.0 44.2 jit_solution(4816435302012089136)
XLA Ops:
  0.6 0.0 copy-start
  0.6 1.6 %copy-done = bf16[128,32,256]{2,1,0:T(8,128)(2,1)S(1)} copy-done((bf16[128,32,256]{2,1,0:T(8,128)(2,1)S(1)}, bf16[128,32,256]{2,1,0:T(8,128)(2,1)}, u32[]{:S(2)}) %copy-start) | copy-done | bytes 2097176
  2.2 0.0 copy-start.1
  2.2 1.6 %copy-done.1 = bf16[128,32,256]{2,1,0:T(8,128)(2,1)S(1)} copy-done((bf16[128,32,256]{2,1,0:T(8,128)(2,1)S(1)}, bf16[128,32,256]{2,1,0:T(8,128)(2,1)}, u32[]{:S(2)}) %copy-start.1) | copy-done | bytes 2097176
  3.8 0.0 copy-start.2
  3.8 0.8 %copy-done.2 = f32[32,256]{1,0:T(8,128)S(1)} copy-done((f32[32,256]{1,0:T(8,128)S(1)}, f32[32,256]{1,0:T(8,128)}, u32[]{:S(2)}) %copy-start.2) | copy-done | bytes 32792
  4.6 0.0 copy-start.3
  4.6 0.8 %copy-done.3 = f32[32,256]{1,0:T(8,128)S(1)} copy-done((f32[32,256]{1,0:T(8,128)S(1)}, f32[32,256]{1,0:T(8,128)}, u32[]{:S(2)}) %copy-start.3) | copy-done | bytes 32792
  5.3 34.8 %filter.1 = (bf16[32,256,256]{2,1,0:T(8,128)(2,1)S(1)}, bf16[256,256]{1,0:T(8,128)(2,1)S(1)}) custom-call(bf16[128,32,256]{2,1,0:T(8,128)(2,1)S(1)} %copy-done, bf16[128,32,256]{2,1,0:T(8,128)(2,1)S(1)} %copy-done.1, f32[32,256]{1,0:T(8,128)S(1)} %copy-done.2, f32[32,256]{1,0:T(8,128)S(1)} %copy-done.3), custom_call_target="tpu_custom_call" | custom-call | tf_op jit(solution)/shard_map/filter/pallas_call | solution.py:354
  40.1 4.1 %rebuild.1 = (bf16[128,32,256]{2,1,0:T(8,128)(2,1)}, bf16[128,32,256]{2,1,0:T(8,128)(2,1)}) custom-call(bf16[32,256,256]{2,1,0:T(8,128)(2,1)S(1)} %get-tuple-element.4.s_ref, bf16[256,256]{1,0:T(8,128)(2,1)S(1)} %get-tuple-element.5.filter_ref), custom_call_target="tpu_custom_call" | custom-call | tf_op jit(solution)/shard_map/rebuild/pallas_call | solution.py:395
Async XLA Ops:
  0.6 1.6 %copy-start = (bf16[128,32,256]{2,1,0:T(8,128)(2,1)S(1)}, bf16[128,32,256]{2,1,0:T(8,128)(2,1)}, u32[]{:S(2)}) copy-start(bf16[128,32,256]{2,1,0:T(8,128)(2,1)} %u_hbm.1) | copy-start | bytes 6291460
  2.2 1.6 %copy-start.1 = (bf16[128,32,256]{2,1,0:T(8,128)(2,1)S(1)}, bf16[128,32,256]{2,1,0:T(8,128)(2,1)}, u32[]{:S(2)}) copy-start(bf16[128,32,256]{2,1,0:T(8,128)(2,1)} %v_hbm.1) | copy-start | bytes 6291460
  3.8 0.8 %copy-start.2 = (f32[32,256]{1,0:T(8,128)S(1)}, f32[32,256]{1,0:T(8,128)}, u32[]{:S(2)}) copy-start(f32[32,256]{1,0:T(8,128)} %idx_hbm.1) | copy-start | bytes 98308
  4.6 0.8 %copy-start.3 = (f32[32,256]{1,0:T(8,128)S(1)}, f32[32,256]{1,0:T(8,128)}, u32[]{:S(2)}) copy-start(f32[32,256]{1,0:T(8,128)} %idy_hbm.1) | copy-start | bytes 98308

commit v2 on v1

--- a/solution.py
+++ b/solution.py
@@ -11,6 +11,7 @@
 EDGE = 2
 SUB = 16
 BATCH = 4
+VMEM_BYTES = 60 * 2**20
 F32 = jnp.float32
 BF16 = jnp.bfloat16
 MESH = pl.DeviceIdType.MESH
@@ -105,13 +106,14 @@
     n_gx, n_gy, snaps, tile_x, tile_y, rows,
     u_hbm, v_hbm, idx_hbm, idy_hbm,
     s_hbm, filter_ref,
-    uv, inv, field, snap, strip, strip_low, strip_high, gram,
+    uv, inv, field, partial, snap, strip, strip_low, strip_high, gram,
     packed, reduce_buf, z_buf, full,
     load_sem, store_sem, x_send, x_recv, y_send, y_recv,
     rs_send, rs_recv, z_send, z_recv, ag_send, ag_recv,
 ):
     gx, gy = lax.axis_index("gx"), lax.axis_index("gy")
     lanes = strip.shape[1]
+    used = -(-(2 * snaps + 8) // rows)
 
     loads = [
         pltpu.make_async_copy(source, target, load_sem.at[i])
@@ -220,6 +222,24 @@
     outer = jnp.where(spot >= lanes // 2, -EDGE, tile_y) + spot % EDGE
     beyond = stencil_weight(outer - iota((lanes, tile_y), 1))
 
+    def inland(x0, count):
+        middle = field[pl.ds(x0 + EDGE, count)].reshape(count * 2 * snaps, tile_y)
+        along_y = dot(middle, within)
+        for i in range(count):
+            near = field[x0 + i + 3].astype(F32) - field[x0 + i + 1].astype(F32)
+            far = field[x0 + i].astype(F32) - field[x0 + i + 4].astype(F32)
+            along_x = far + 8.0 * near
+            at = along_y[i * 2 * snaps : (i + 1) * 2 * snaps]
+            idx, idy = inv[0, pl.ds(x0 + i, 1), :], inv[1, pl.ds(x0 + i, 1), :]
+            partial[x0 + i, :snaps] = idx * along_x[snaps:] - idy * at[:snaps]
+            partial[x0 + i, snaps:] = idx * along_x[:snaps] + idy * at[snaps:]
+
+    def interior(step, carry):
+        inland(EDGE + step * BATCH, BATCH)
+        return carry
+
+    lax.fori_loop(0, (tile_x - 2 * EDGE) // BATCH, interior, 0)
+
     def wait_arrivals(copy, index, count):
         for comp in range(2):
             for up in range(2):
@@ -227,42 +247,35 @@
                 def _(comp=comp, up=up):
                     copy(comp, up).wait_recv()
 
+    wait_arrivals(x_copy, gx, n_gx)
+    inland(0, EDGE)
+    inland(tile_x - EDGE, EDGE)
     wait_arrivals(y_copy, gy, n_gy)
     wide = (2 * snaps, lanes)
     halo = jnp.where(
         iota(wide, 1) >= lanes // 2, strip_low[...].astype(F32), strip_high[...].astype(F32)
     )
+    halo = jnp.where(iota(wide, 0) < snaps, -halo, halo)
     strip_low[...] = halo.astype(BF16)
     owner = (iota(wide, 1) % (lanes // 2)) // EDGE
 
-    def fields(x0, count):
-        middle = field[pl.ds(x0 + EDGE, count)].reshape(count * 2 * snaps, tile_y)
+    def finish(step, carry):
+        x0 = step * BATCH
         side = strip_low[...].astype(F32)
-        sides = [jnp.where(owner == x0 + i, side, 0.0).astype(BF16) for i in range(count)]
-        along_y = dot(middle, within) + dot(jnp.concatenate(sides, axis=0), beyond)
+        sides = [jnp.where(owner == x0 + i, side, 0.0).astype(BF16) for i in range(BATCH)]
+        rest = dot(jnp.concatenate(sides, axis=0), beyond)
         done = []
-        for i in range(count):
-            near = field[x0 + i + 3].astype(F32) - field[x0 + i + 1].astype(F32)
-            far = field[x0 + i].astype(F32) - field[x0 + i + 4].astype(F32)
-            along_x = far + 8.0 * near
-            at = along_y[i * 2 * snaps : (i + 1) * 2 * snaps]
-            idx, idy = inv[0, pl.ds(x0 + i, 1), :], inv[1, pl.ds(x0 + i, 1), :]
-            vorticity = idx * along_x[snaps:] - idy * at[:snaps]
-            divergence = idx * along_x[:snaps] + idy * at[snaps:]
-            both = jnp.concatenate([vorticity, divergence], axis=0).astype(BF16)
+        for i in range(BATCH):
+            idy = inv[1, pl.ds(x0 + i, 1), :]
+            both = partial[x0 + i] + idy * rest[i * 2 * snaps : (i + 1) * 2 * snaps]
+            both = both.astype(BF16)
             snap[x0 + i] = both
             done.append(both)
         flat = jnp.concatenate(done, axis=1)
         gram[...] += dot_nt(flat, flat)
-
-    def interior(step, carry):
-        fields(EDGE + step * BATCH, BATCH)
         return carry
 
-    lax.fori_loop(0, (tile_x - 2 * EDGE) // BATCH, interior, 0)
-    wait_arrivals(x_copy, gx, n_gx)
-    fields(0, EDGE)
-    fields(tile_x - EDGE, EDGE)
+    lax.fori_loop(0, tile_x // BATCH, finish, 0)
 
     store = pltpu.make_async_copy(snap, s_hbm, store_sem)
     store.start()
@@ -291,25 +304,38 @@
             device_id={"gx": lax.rem(gx + k, n_gx)}, device_id_type=MESH,
         )
 
+    def owns(peer):
+        return peer < used
+
     for k in range(1, n_gx):
-        rs_copy(k).start()
-    mine = packed[gx]
+        @pl.when(owns(lax.rem(gx + k, n_gx)))
+        def _(k=k):
+            rs_copy(k).start()
+
+    @pl.when(owns(gx))
+    def _():
+        mine = packed[gx]
+        for k in range(1, n_gx):
+            rs_copy(k).wait_recv()
+            mine = mine + reduce_buf[k]
+        z_buf[0] = mine
+        for k in range(1, n_gy):
+            z_copy(k).start()
+        for k in range(1, n_gy):
+            z_copy(k).wait_recv()
+        total = z_buf[gy]
+        for z in range(1, n_gy):
+            total = total + z_buf[lax.rem(gy - z + n_gy, n_gy)]
+        full[gx] = total
+        for k in range(1, n_gx):
+            ag_copy(k, gx).start()
+
     for k in range(1, n_gx):
-        rs_copy(k).wait_recv()
-        mine = mine + reduce_buf[k]
-    z_buf[0] = mine
-    for k in range(1, n_gy):
-        z_copy(k).start()
-    for k in range(1, n_gy):
-        z_copy(k).wait_recv()
-    total = z_buf[lax.rem(gy, n_gy)]
-    for z in range(1, n_gy):
-        total = total + z_buf[lax.rem(gy - z + n_gy, n_gy)]
-    full[gx] = total
-    for k in range(1, n_gx):
-        ag_copy(k, gx).start()
-    for k in range(1, n_gx):
-        ag_copy(k, lax.rem(gx - k + n_gx, n_gx)).wait_recv()
+        sender = lax.rem(gx - k + n_gx, n_gx)
+
+        @pl.when(owns(sender))
+        def _(k=k, sender=sender):
+            ag_copy(k, sender).wait_recv()
 
     filter_ref[...] = spectral_filter(unpack_gram(full[...]))
 
@@ -323,25 +349,56 @@
             def _(comp=comp, up=up):
                 x_copy(comp, up).wait_send()
     for k in range(1, n_gx):
-        rs_copy(k).wait_send()
-        ag_copy(k, gx).wait_send()
-    for k in range(1, n_gy):
-        z_copy(k).wait_send()
+        @pl.when(owns(lax.rem(gx + k, n_gx)))
+        def _(k=k):
+            rs_copy(k).wait_send()
+
+    @pl.when(owns(gx))
+    def _():
+        for k in range(1, n_gx):
+            ag_copy(k, gx).wait_send()
+        for k in range(1, n_gy):
+            z_copy(k).wait_send()
+
     store.wait()
 
 
-def rebuild_kernel(s_ref, filter_ref, vort_ref, div_ref, mixed):
-    count, order, tile_y = s_ref.shape
+def rebuild_kernel(
+    s_hbm, filter_hbm, vort_hbm, div_hbm, snap, filter_ref, mixed, out, filter_sem, in_sem, out_sem
+):
+    tile_x, order, tile_y = snap.shape
     half = order // 2
-    for x in range(count):
-        mixed[x] = dot(filter_ref[...], s_ref[x]).astype(BF16)
+    part = SUB // 2
+    filter_load = pltpu.make_async_copy(filter_hbm, filter_ref, filter_sem)
+    filter_load.start()
+    loads = []
+    for i in range(tile_x // part):
+        span = pl.ds(i * part, part)
+        loads.append(pltpu.make_async_copy(s_hbm.at[span], snap.at[span], in_sem.at[i]))
+        loads[-1].start()
     swap = swap_matrix()
-    for first in range(0, order, SUB):
-        block = mixed[:, first : first + SUB, :].reshape(SUB * SUB, tile_y)
-        back = dot(swap, block).astype(BF16).reshape(SUB, SUB, tile_y)
-        out = vort_ref if first < half else div_ref
-        start = first % half
-        out[start : start + SUB] = back
+    filter_load.wait()
+    stores = []
+    for x0 in range(0, tile_x, SUB):
+        for x in range(x0, x0 + SUB):
+            if x % part == 0:
+                loads[x // part].wait()
+            mixed[x] = dot(filter_ref[...], snap[x]).astype(BF16)
+        for first in range(0, order, SUB):
+            block = mixed[x0 : x0 + SUB, first : first + SUB, :]
+            back = dot(swap, block.reshape(SUB * SUB, tile_y)).astype(BF16)
+            field, start = first // half, first % half
+            where = (pl.ds(start, SUB), pl.ds(x0, SUB))
+            out[field, start : start + SUB, x0 : x0 + SUB, :] = back.reshape(SUB, SUB, tile_y)
+            store = pltpu.make_async_copy(
+                out.at[field].at[where],
+                (vort_hbm, div_hbm)[field].at[where],
+                out_sem.at[x0 // SUB, first // SUB],
+            )
+            store.start()
+            stores.append(store)
+    for store in stores:
+        store.wait()
 
 
 def per_device(n_gx, n_gy, u_vel, v_vel, inv_dx, inv_dy):
@@ -363,6 +420,7 @@
             pltpu.VMEM((2, snaps, tile_x, tile_y), BF16),
             pltpu.VMEM((2, tile_x, tile_y), F32),
             pltpu.VMEM((tile_x + 2 * EDGE, order, tile_y), BF16),
+            pltpu.VMEM((tile_x, order, tile_y), F32),
             pltpu.VMEM((tile_x, order, tile_y), BF16),
             pltpu.VMEM((order, lanes), BF16),
             pltpu.VMEM((order, lanes), BF16),
@@ -386,23 +444,26 @@
             dma((n_gx,)),
         ],
         compiler_params=pltpu.CompilerParams(
-            collective_id=0, has_side_effects=True, vmem_limit_bytes=40 * 2**20
+            collective_id=0, has_side_effects=True, vmem_limit_bytes=VMEM_BYTES
         ),
         name="filter",
     )(u_vel, v_vel, inv_dx, inv_dy)
     out = jax.ShapeDtypeStruct((snaps, tile_x, tile_y), BF16)
-    block = pl.BlockSpec((snaps, SUB, tile_y), lambda i: (0, i, 0))
     return pl.pallas_call(
         rebuild_kernel,
         out_shape=(out, out),
-        grid=(tile_x // SUB,),
-        in_specs=[
-            pl.BlockSpec((SUB, order, tile_y), lambda i: (i, 0, 0)),
-            pl.BlockSpec((order, order), lambda i: (0, 0)),
+        in_specs=[any_spec, any_spec],
+        out_specs=(any_spec, any_spec),
+        scratch_shapes=[
+            pltpu.VMEM((tile_x, order, tile_y), BF16),
+            pltpu.VMEM((order, order), BF16),
+            pltpu.VMEM((tile_x, order, tile_y), BF16),
+            pltpu.VMEM((2, snaps, tile_x, tile_y), BF16),
+            dma,
+            dma((2 * tile_x // SUB,)),
+            dma((tile_x // SUB, order // SUB)),
         ],
-        out_specs=(block, block),
-        scratch_shapes=[pltpu.VMEM((SUB, order, tile_y), BF16)],
-        compiler_params=pltpu.CompilerParams(vmem_limit_bytes=40 * 2**20),
+        compiler_params=pltpu.CompilerParams(vmem_limit_bytes=VMEM_BYTES),
         name="rebuild",
     )(snapshots, spectral)
 

time: 44.5 us -> 43 us (0.966)
  local copies, waits for them, and re-layouts: 4.69 us -> 0 us
  Pallas kernels: 38.9 us -> 42.3 us
    unnamed x8 -> x0, local copies, waits for them, and re-layouts: 4.69 us -> none
    pallas_call x1, Pallas kernels: 4.07 us -> 6.03 us  [per_device(): pl.pallas_call(rebuild_kernel, out_shape=(out, out), in_specs=[any_spec,...]
    pallas_call x1, Pallas kernels: 34.8 us -> 36.2 us  [per_device(): pl.pallas_call(functools.partial(filter_kernel, n_gx, n_gy, snaps, tile_x...]
where the time goes in v2:
time: 43 us; the launch traced here: 42.9 us
  Pallas kernels  42.3 us (98%)
  between operations  0.64 us (1%)
    pallas_call x1, Pallas kernels, per_device(): pl.pallas_call(functools.partial(filter_kernel, n_gx, n_gy, snaps, tile_x...  36.2 us
    pallas_call x1, Pallas kernels, per_device(): pl.pallas_call(rebuild_kernel, out_shape=(out, out), in_specs=[any_spec,...  6.03 us

profile of v2, /device:TPU:0, one launch (start us, length us, event | category | flops | bytes accessed | tf_op | source)
XLA Modules:
  0.0 42.9 jit_solution(8799101658990113997)
XLA Ops:
  0.6 36.2 %filter.1 = (bf16[32,256,256]{2,1,0:T(8,128)(2,1)}, bf16[256,256]{1,0:T(8,128)(2,1)}) custom-call(bf16[128,32,256]{2,1,0:T(8,128)(2,1)} %u_hbm.1, bf16[128,32,256]{2,1,0:T(8,128)(2,1)} %v_hbm.1, f32[32,256]{1,0:T(8,128)} %idx_hbm.1, f32[32,256]{1,0:T(8,128)} %idy_hbm.1), custom_call_target="tpu_custom_call" | custom-call | tf_op jit(solution)/shard_map/filter/pallas_call | solution.py:411
  36.9 6.0 %rebuild.1 = (bf16[128,32,256]{2,1,0:T(8,128)(2,1)}, bf16[128,32,256]{2,1,0:T(8,128)(2,1)}) custom-call(bf16[32,256,256]{2,1,0:T(8,128)(2,1)} %get-tuple-element.4.s_hbm, bf16[256,256]{1,0:T(8,128)(2,1)} %get-tuple-element.5.filter_hbm), custom_call_target="tpu_custom_call" | custom-call | tf_op jit(solution)/shard_map/rebuild/pallas_call | solution.py:452

commit v3 on v2

--- a/solution.py
+++ b/solution.py
@@ -115,12 +115,14 @@
     lanes = strip.shape[1]
     used = -(-(2 * snaps + 8) // rows)
 
-    loads = [
-        pltpu.make_async_copy(source, target, load_sem.at[i])
-        for i, (source, target) in enumerate(
-            [(u_hbm, uv.at[0]), (v_hbm, uv.at[1]), (idx_hbm, inv.at[0]), (idy_hbm, inv.at[1])]
-        )
-    ]
+    span = SUB * BATCH
+    loads = []
+    for comp, source in enumerate((u_hbm, v_hbm)):
+        for first in range(0, snaps, span):
+            at = pl.ds(first, span)
+            loads.append((source.at[at], uv.at[comp, at]))
+    loads += [(idx_hbm, inv.at[0]), (idy_hbm, inv.at[1])]
+    loads = [pltpu.make_async_copy(*pair, load_sem.at[i]) for i, pair in enumerate(loads)]
     for load in loads:
         load.start()
 
@@ -164,8 +166,7 @@
     lane_x = (iota(group, 2) % (lanes // 2)) // EDGE - iota(group, 0)
 
     def permute(comp, j):
-        first = pl.multiple_of(j * SUB, SUB)
-        there = pl.multiple_of(comp * snaps + j * SUB, SUB)
+        first, there = j * SUB, comp * snaps + j * SUB
         edge = jnp.zeros((SUB, lanes), F32)
         for x0 in range(0, tile_x, SUB):
             block = uv[comp, pl.ds(first, SUB), x0 : x0 + SUB, :]
@@ -178,14 +179,11 @@
         strip[pl.ds(there, SUB), :] = edge.astype(BF16)
 
     for comp in range(2):
-        loads[comp].wait()
-
-        def permute_some(step, carry, comp=comp):
+        steps = snaps // span
+        for step in range(steps):
+            loads[comp * steps + step].wait()
             for i in range(BATCH):
                 permute(comp, step * BATCH + i)
-            return carry
-
-        lax.fori_loop(0, snaps // SUB // BATCH, permute_some, 0)
         if comp == 0:
             pl.semaphore_wait(barrier, n_gx + n_gy - 2)
         for up in range(2):
@@ -213,7 +211,7 @@
     def _():
         strip_high[...] = jnp.zeros((2 * snaps, lanes), BF16)
 
-    for load in loads[2:]:
+    for load in loads[-2:]:
         load.wait()
     inv[...] = inv[...] * (1.0 / 12.0)
     gram[...] = jnp.zeros_like(gram)
@@ -282,60 +280,68 @@
 
     packed[...] = pack_gram(gram[...], rows, n_gx)
 
-    def rs_copy(k):
+    cut = -(-rows // 16) * 8
+    spans = [pl.ds(0, cut), pl.ds(cut, rows - cut)] if cut < rows else [pl.ds(0, rows)]
+    pieces = range(len(spans))
+
+    def rs_copy(p, k):
         peer = lax.rem(gx + k, n_gx)
         return pltpu.make_async_remote_copy(
-            src_ref=packed.at[peer], dst_ref=reduce_buf.at[k],
-            send_sem=rs_send.at[k], recv_sem=rs_recv.at[k],
+            src_ref=packed.at[peer, spans[p]], dst_ref=reduce_buf.at[k, spans[p]],
+            send_sem=rs_send.at[p, k], recv_sem=rs_recv.at[p, k],
             device_id={"gx": peer}, device_id_type=MESH,
         )
 
-    def z_copy(k):
+    def z_copy(p, k):
         return pltpu.make_async_remote_copy(
-            src_ref=z_buf.at[0], dst_ref=z_buf.at[k],
-            send_sem=z_send.at[k], recv_sem=z_recv.at[k],
+            src_ref=z_buf.at[0, spans[p]], dst_ref=z_buf.at[k, spans[p]],
+            send_sem=z_send.at[p, k], recv_sem=z_recv.at[p, k],
             device_id={"gy": lax.rem(gy + k, n_gy)}, device_id_type=MESH,
         )
 
-    def ag_copy(k, block):
+    def ag_copy(p, k, block):
         return pltpu.make_async_remote_copy(
-            src_ref=full.at[block], dst_ref=full.at[block],
-            send_sem=ag_send.at[k], recv_sem=ag_recv.at[k],
+            src_ref=full.at[block, spans[p]], dst_ref=full.at[block, spans[p]],
+            send_sem=ag_send.at[p, k], recv_sem=ag_recv.at[p, k],
             device_id={"gx": lax.rem(gx + k, n_gx)}, device_id_type=MESH,
         )
 
     def owns(peer):
         return peer < used
 
-    for k in range(1, n_gx):
-        @pl.when(owns(lax.rem(gx + k, n_gx)))
-        def _(k=k):
-            rs_copy(k).start()
+    for p in pieces:
+        for k in range(1, n_gx):
+            @pl.when(owns(lax.rem(gx + k, n_gx)))
+            def _(p=p, k=k):
+                rs_copy(p, k).start()
 
     @pl.when(owns(gx))
     def _():
-        mine = packed[gx]
+        for p in pieces:
+            mine = packed[gx, spans[p]]
+            for k in range(1, n_gx):
+                rs_copy(p, k).wait_recv()
+                mine = mine + reduce_buf[k, spans[p]]
+            z_buf[0, spans[p]] = mine
+            for k in range(1, n_gy):
+                z_copy(p, k).start()
+        for p in pieces:
+            for k in range(1, n_gy):
+                z_copy(p, k).wait_recv()
+            total = z_buf[gy, spans[p]]
+            for z in range(1, n_gy):
+                total = total + z_buf[lax.rem(gy - z + n_gy, n_gy), spans[p]]
+            full[gx, spans[p]] = total
+            for k in range(1, n_gx):
+                ag_copy(p, k, gx).start()
+
+    for p in pieces:
         for k in range(1, n_gx):
-            rs_copy(k).wait_recv()
-            mine = mine + reduce_buf[k]
-        z_buf[0] = mine
-        for k in range(1, n_gy):
-            z_copy(k).start()
-        for k in range(1, n_gy):
-            z_copy(k).wait_recv()
-        total = z_buf[gy]
-        for z in range(1, n_gy):
-            total = total + z_buf[lax.rem(gy - z + n_gy, n_gy)]
-        full[gx] = total
-        for k in range(1, n_gx):
-            ag_copy(k, gx).start()
-
-    for k in range(1, n_gx):
-        sender = lax.rem(gx - k + n_gx, n_gx)
-
-        @pl.when(owns(sender))
-        def _(k=k, sender=sender):
-            ag_copy(k, sender).wait_recv()
+            sender = lax.rem(gx - k + n_gx, n_gx)
+
+            @pl.when(owns(sender))
+            def _(p=p, k=k, sender=sender):
+                ag_copy(p, k, sender).wait_recv()
 
     filter_ref[...] = spectral_filter(unpack_gram(full[...]))
 
@@ -348,17 +354,19 @@
             @pl.when(has(gx, n_gx, up))
             def _(comp=comp, up=up):
                 x_copy(comp, up).wait_send()
-    for k in range(1, n_gx):
-        @pl.when(owns(lax.rem(gx + k, n_gx)))
-        def _(k=k):
-            rs_copy(k).wait_send()
+    for p in pieces:
+        for k in range(1, n_gx):
+            @pl.when(owns(lax.rem(gx + k, n_gx)))
+            def _(p=p, k=k):
+                rs_copy(p, k).wait_send()
 
     @pl.when(owns(gx))
     def _():
-        for k in range(1, n_gx):
-            ag_copy(k, gx).wait_send()
-        for k in range(1, n_gy):
-            z_copy(k).wait_send()
+        for p in pieces:
+            for k in range(1, n_gx):
+                ag_copy(p, k, gx).wait_send()
+            for k in range(1, n_gy):
+                z_copy(p, k).wait_send()
 
     store.wait()
 
@@ -388,15 +396,16 @@
             block = mixed[x0 : x0 + SUB, first : first + SUB, :]
             back = dot(swap, block.reshape(SUB * SUB, tile_y)).astype(BF16)
             field, start = first // half, first % half
-            where = (pl.ds(start, SUB), pl.ds(x0, SUB))
             out[field, start : start + SUB, x0 : x0 + SUB, :] = back.reshape(SUB, SUB, tile_y)
-            store = pltpu.make_async_copy(
-                out.at[field].at[where],
-                (vort_hbm, div_hbm)[field].at[where],
-                out_sem.at[x0 // SUB, first // SUB],
-            )
-            store.start()
-            stores.append(store)
+            if start + SUB == half:
+                span = pl.ds(x0, SUB)
+                store = pltpu.make_async_copy(
+                    out.at[field, :, span],
+                    (vort_hbm, div_hbm)[field].at[:, span],
+                    out_sem.at[x0 // SUB, field],
+                )
+                store.start()
+                stores.append(store)
     for store in stores:
         store.wait()
 
@@ -430,18 +439,18 @@
             pltpu.VMEM((n_gx, rows, snaps), F32),
             pltpu.VMEM((n_gy, rows, snaps), F32),
             pltpu.VMEM((n_gx, rows, snaps), F32),
-            dma((4,)),
+            dma((2 * snaps // (SUB * BATCH) + 2,)),
             dma,
             dma((2, 2)),
             dma((2, 2)),
             dma((2, 2)),
             dma((2, 2)),
-            dma((n_gx,)),
-            dma((n_gx,)),
-            dma((n_gy,)),
-            dma((n_gy,)),
-            dma((n_gx,)),
-            dma((n_gx,)),
+            dma((2, n_gx)),
+            dma((2, n_gx)),
+            dma((2, n_gy)),
+            dma((2, n_gy)),
+            dma((2, n_gx)),
+            dma((2, n_gx)),
         ],
         compiler_params=pltpu.CompilerParams(
             collective_id=0, has_side_effects=True, vmem_limit_bytes=VMEM_BYTES
@@ -461,7 +470,7 @@
             pltpu.VMEM((2, snaps, tile_x, tile_y), BF16),
             dma,
             dma((2 * tile_x // SUB,)),
-            dma((tile_x // SUB, order // SUB)),
+            dma((tile_x // SUB, 2)),
         ],
         compiler_params=pltpu.CompilerParams(vmem_limit_bytes=VMEM_BYTES),
         name="rebuild",

time: 43 us -> 42.8 us (level)
  no operation moved by 1% of the time
where the time goes in v3:
time: 42.8 us; the launch traced here: 42.6 us
  Pallas kernels  42 us (98%)
  between operations  0.64 us (1%)
    pallas_call x1, Pallas kernels, per_device(): pl.pallas_call(functools.partial(filter_kernel, n_gx, n_gy, snaps, tile_x...  36 us
    pallas_call x1, Pallas kernels, per_device(): pl.pallas_call(rebuild_kernel, out_shape=(out, out), in_specs=[any_spec,...  5.98 us

profile of v3, /device:TPU:0, one launch (start us, length us, event | category | flops | bytes accessed | tf_op | source)
XLA Modules:
  0.0 42.6 jit_solution(16549078354830653303)
XLA Ops:
  0.6 36.0 %filter.1 = (bf16[32,256,256]{2,1,0:T(8,128)(2,1)}, bf16[256,256]{1,0:T(8,128)(2,1)}) custom-call(bf16[128,32,256]{2,1,0:T(8,128)(2,1)} %u_hbm.1, bf16[128,32,256]{2,1,0:T(8,128)(2,1)} %v_hbm.1, f32[32,256]{1,0:T(8,128)} %idx_hbm.1, f32[32,256]{1,0:T(8,128)} %idy_hbm.1), custom_call_target="tpu_custom_call" | custom-call | tf_op jit(solution)/shard_map/filter/pallas_call | solution.py:420
  36.6 6.0 %rebuild.1 = (bf16[128,32,256]{2,1,0:T(8,128)(2,1)}, bf16[128,32,256]{2,1,0:T(8,128)(2,1)}) custom-call(bf16[32,256,256]{2,1,0:T(8,128)(2,1)} %get-tuple-element.4.s_hbm, bf16[256,256]{1,0:T(8,128)(2,1)} %get-tuple-element.5.filter_hbm), custom_call_target="tpu_custom_call" | custom-call | tf_op jit(solution)/shard_map/rebuild/pallas_call | solution.py:461

commit v4 on v3

--- a/solution.py
+++ b/solution.py
@@ -11,7 +11,8 @@
 EDGE = 2
 SUB = 16
 BATCH = 4
-VMEM_BYTES = 60 * 2**20
+PARTS = 4
+VMEM_BYTES = 48 * 2**20
 F32 = jnp.float32
 BF16 = jnp.bfloat16
 MESH = pl.DeviceIdType.MESH
@@ -105,7 +106,7 @@
 def filter_kernel(
     n_gx, n_gy, snaps, tile_x, tile_y, rows,
     u_hbm, v_hbm, idx_hbm, idy_hbm,
-    s_hbm, filter_ref,
+    s_parts, filter_ref,
     uv, inv, field, partial, snap, strip, strip_low, strip_high, gram,
     packed, reduce_buf, z_buf, full,
     load_sem, store_sem, x_send, x_recv, y_send, y_recv,
@@ -275,8 +276,13 @@
 
     lax.fori_loop(0, tile_x // BATCH, finish, 0)
 
-    store = pltpu.make_async_copy(snap, s_hbm, store_sem)
-    store.start()
+    part = tile_x // len(s_parts)
+    stores = [
+        pltpu.make_async_copy(snap.at[pl.ds(i * part, part)], s_part, store_sem.at[i])
+        for i, s_part in enumerate(s_parts)
+    ]
+    for store in stores:
+        store.start()
 
     packed[...] = pack_gram(gram[...], rows, n_gx)
 
@@ -368,30 +374,21 @@
             for k in range(1, n_gy):
                 z_copy(p, k).wait_send()
 
-    store.wait()
+    for store in stores:
+        store.wait()
 
 
 def rebuild_kernel(
-    s_hbm, filter_hbm, vort_hbm, div_hbm, snap, filter_ref, mixed, out, filter_sem, in_sem, out_sem
+    s_parts, filter_ref, vort_hbm, div_hbm, mixed, out, out_sem
 ):
-    tile_x, order, tile_y = snap.shape
+    tile_x, order, tile_y = mixed.shape
+    part = tile_x // len(s_parts)
     half = order // 2
-    part = SUB // 2
-    filter_load = pltpu.make_async_copy(filter_hbm, filter_ref, filter_sem)
-    filter_load.start()
-    loads = []
-    for i in range(tile_x // part):
-        span = pl.ds(i * part, part)
-        loads.append(pltpu.make_async_copy(s_hbm.at[span], snap.at[span], in_sem.at[i]))
-        loads[-1].start()
     swap = swap_matrix()
-    filter_load.wait()
     stores = []
     for x0 in range(0, tile_x, SUB):
         for x in range(x0, x0 + SUB):
-            if x % part == 0:
-                loads[x // part].wait()
-            mixed[x] = dot(filter_ref[...], snap[x]).astype(BF16)
+            mixed[x] = dot(filter_ref[...], s_parts[x // part][x % part]).astype(BF16)
         for first in range(0, order, SUB):
             block = mixed[x0 : x0 + SUB, first : first + SUB, :]
             back = dot(swap, block.reshape(SUB * SUB, tile_y)).astype(BF16)
@@ -420,11 +417,11 @@
     snapshots, spectral = pl.pallas_call(
         functools.partial(filter_kernel, n_gx, n_gy, snaps, tile_x, tile_y, rows),
         out_shape=(
-            jax.ShapeDtypeStruct((tile_x, order, tile_y), BF16),
+            [jax.ShapeDtypeStruct((tile_x // PARTS, order, tile_y), BF16)] * PARTS,
             jax.ShapeDtypeStruct((order, order), BF16),
         ),
         in_specs=[any_spec] * 4,
-        out_specs=(any_spec, pl.BlockSpec(memory_space=pltpu.VMEM)),
+        out_specs=([any_spec] * PARTS, pl.BlockSpec(memory_space=pltpu.VMEM)),
         scratch_shapes=[
             pltpu.VMEM((2, snaps, tile_x, tile_y), BF16),
             pltpu.VMEM((2, tile_x, tile_y), F32),
@@ -440,7 +437,7 @@
             pltpu.VMEM((n_gy, rows, snaps), F32),
             pltpu.VMEM((n_gx, rows, snaps), F32),
             dma((2 * snaps // (SUB * BATCH) + 2,)),
-            dma,
+            dma((PARTS,)),
             dma((2, 2)),
             dma((2, 2)),
             dma((2, 2)),
@@ -461,18 +458,14 @@
     return pl.pallas_call(
         rebuild_kernel,
         out_shape=(out, out),
-        in_specs=[any_spec, any_spec],
+        in_specs=[[pl.BlockSpec(memory_space=pltpu.VMEM)] * PARTS, pl.BlockSpec(memory_space=pltpu.VMEM)],
         out_specs=(any_spec, any_spec),
         scratch_shapes=[
             pltpu.VMEM((tile_x, order, tile_y), BF16),
-            pltpu.VMEM((order, order), BF16),
-            pltpu.VMEM((tile_x, order, tile_y), BF16),
             pltpu.VMEM((2, snaps, tile_x, tile_y), BF16),
-            dma,
-            dma((2 * tile_x // SUB,)),
             dma((tile_x // SUB, 2)),
         ],
-        compiler_params=pltpu.CompilerParams(vmem_limit_bytes=VMEM_BYTES),
+        compiler_params=pltpu.CompilerParams(vmem_limit_bytes=30 * 2**20),
         name="rebuild",
     )(snapshots, spectral)
 

time: 42.8 us -> 41.7 us (0.974)
  Pallas kernels: 42 us -> 39.3 us
  local copies, waits for them, and re-layouts: 0 us -> 1.51 us
    pallas_call x1, Pallas kernels: 5.98 us -> 3.6 us  [per_device(): pl.pallas_call(rebuild_kernel, out_shape=(out, out), in_specs=[[pl.BlockS...]
    unnamed x0 -> x4, local copies, waits for them, and re-layouts: none -> 1.51 us
where the time goes in v4:
time: 41.7 us; the launch traced here: 41.4 us
  Pallas kernels  39.3 us (94%)
  local copies, waits for them, and re-layouts  1.51 us (4%)
  between operations  0.65 us (2%)
    pallas_call x1, Pallas kernels, per_device(): pl.pallas_call(functools.partial(filter_kernel, n_gx, n_gy, snaps, tile_x...  35.7 us
    pallas_call x1, Pallas kernels, per_device(): pl.pallas_call(rebuild_kernel, out_shape=(out, out), in_specs=[[pl.BlockS...  3.6 us
    unnamed x4, local copies, waits for them, and re-layouts  1.51 us

profile of v4, /device:TPU:0, one launch (start us, length us, event | category | flops | bytes accessed | tf_op | source)
XLA Modules:
  0.0 41.4 jit_solution(1848977495313560629)
XLA Ops:
  0.6 0.0 copy-start
  0.6 0.7 %copy-done = f32[32,256]{1,0:T(8,128)S(1)} copy-done((f32[32,256]{1,0:T(8,128)S(1)}, f32[32,256]{1,0:T(8,128)}, u32[]{:S(2)}) %copy-start) | copy-done | bytes 32792
  1.4 0.0 copy-start.1
  1.4 0.8 %copy-done.1 = f32[32,256]{1,0:T(8,128)S(1)} copy-done((f32[32,256]{1,0:T(8,128)S(1)}, f32[32,256]{1,0:T(8,128)}, u32[]{:S(2)}) %copy-start.1) | copy-done | bytes 32792
  2.1 35.7 %filter.1 = (bf16[8,256,256]{2,1,0:T(8,128)(2,1)S(1)}, bf16[8,256,256]{2,1,0:T(8,128)(2,1)S(1)}, bf16[8,256,256]{2,1,0:T(8,128)(2,1)S(1)}, bf16[8,256,256]{2,1,0:T(8,128)(2,1)S(1)}, bf16[256,256]{1,0:T(8,128)(2,1)S(1)}) custom-call(bf16[128,32,256]{2,1,0:T(8,128)(2,1)} %u_hbm.1, bf16[128,32,256]{2,1,0:T(8,128)(2,1)} %v_hbm.1, f32[32,256]{1,0:T(8,128)S(1)} %copy-done, ...), custom_call_target="tpu_custom_call" | custom-call | tf_op jit(solution)/shard_map/filter/pallas_call | solution.py:417
  37.8 3.6 %rebuild.1 = (bf16[128,32,256]{2,1,0:T(8,128)(2,1)}, bf16[128,32,256]{2,1,0:T(8,128)(2,1)}) custom-call(bf16[8,256,256]{2,1,0:T(8,128)(2,1)S(1)} %get-tuple-element.7.s_parts_0_, bf16[8,256,256]{2,1,0:T(8,128)(2,1)S(1)} %get-tuple-element.8.s_parts_1_, bf16[8,256,256]{2,1,0:T(8,128)(2,1)S(1)} %get-tuple-element.9.s_parts_2_, ...), custom_call_target="tpu_custom_call" | custom-call | tf_op jit(solution)/shard_map/rebuild/pallas_call | solution.py:458
Async XLA Ops:
  0.6 0.8 %copy-start = (f32[32,256]{1,0:T(8,128)S(1)}, f32[32,256]{1,0:T(8,128)}, u32[]{:S(2)}) copy-start(f32[32,256]{1,0:T(8,128)} %idx_hbm.1) | copy-start | bytes 98308
  1.4 0.8 %copy-start.1 = (f32[32,256]{1,0:T(8,128)S(1)}, f32[32,256]{1,0:T(8,128)}, u32[]{:S(2)}) copy-start(f32[32,256]{1,0:T(8,128)} %idy_hbm.1) | copy-start | bytes 98308
